TPU v7x, 32 devices: a whole 2x2x4 slice. The times are simulated.
32 devices in a mesh: seq: 16 (over z, y, core), chan: 2 (over x).
Axes of the slice: x: 2, y: 2, z: 4, core: 2. Of those that a mesh axis runs over, the one named last changes fastest.
Arguments:
- tokens: bfloat16 [4096, 512], P('seq', 'chan'), may hold values from -6 to 6
- out_grad: bfloat16 [4096, 512], P('seq', 'chan'), may hold values from -6 to 6
- in_weight: bfloat16 [512, 1024], P('seq', 'chan'), may hold values from -0.25 to 0.25
- dt_weight: bfloat16 [512, 16], P('seq', 'chan'), may hold values from -0.25 to 0.25
- bc_weight: bfloat16 [512, 128], P('seq'), may hold values from -0.0625 to 0.0625
- out_weight: bfloat16 [1024, 512], P('chan', 'seq'), may hold values from -0.1875 to 0.1875
- decay_rate: float32 [2, 16], P(None, 'chan'), may hold values from 0.0014648438 to 8
- dt_bias: float32 [2, 16], P(None, 'chan'), may hold values from -5 to -4
- skip_gain: float32 [16], P('chan'), may hold values from 0.5 to 1.5
Outputs:
- tokens_grad: bfloat16 [4096, 512], P('seq', 'chan')
- in_weight_grad: float32 [512, 1024], P('seq', 'chan')
- dt_weight_grad: float32 [512, 16], P('seq', 'chan')
- bc_weight_grad: float32 [512, 128], P('seq')
- out_weight_grad: float32 [1024, 512], P('chan', 'seq')
- rate_grad: float32 [2, 16], P(None, 'chan')
- bias_grad: float32 [2, 16], P(None, 'chan')
- skip_grad: float32 [16], P('chan')
All inputs are finite; a program needn't handle non-finite values.
Results may differ from a plain program's by a relative error of at most 0.0034.
Values may be sent and summed in bfloat16 or wider, within the bound.
A program may use at most 64 MiB of HBM per device.

v0:
```python
import jax
import jax.numpy as jnp
from jax import lax
from jax.sharding import PartitionSpec as P

STATE = 64
GROUP = 256


def carried_in(value, axis, join, neutral, backward):
    count, mine = (lax.axis_size(axis), lax.axis_index(axis))
    pieces = jax.tree.map(lambda part: lax.all_gather(part, axis), value)
    if backward:
        pieces = jax.tree.map(lambda part: part[::-1], pieces)
        mine = count - 1 - mine
    running = jax.tree.map(
        lambda part, zero: jnp.full_like(part, 0) + jnp.asarray(zero, part.dtype), value, neutral
    )

    def step(position, running):
        longer = join(running, jax.tree.map(lambda part: part[position], pieces))
        return jax.tree.map(lambda new, old: jnp.where(position < mine, new, old), longer, running)

    return lax.fori_loop(0, count - 1, step, running)


def ssd_core(gated, step_size, b_proj, c_proj, rate, skip_gain, start_state):
    length, width = gated.shape
    heads = step_size.shape[1]
    head_dim = width // heads
    blocks = length // GROUP
    log_decay = -rate[None, :] * step_size
    driven = gated.reshape(length, heads, head_dim) * step_size[:, :, None]
    causal = lax.broadcasted_iota(jnp.int32, (GROUP, GROUP), 0) >= lax.broadcasted_iota(
        jnp.int32, (GROUP, GROUP), 1
    )

    def advance(memory, block):
        plain, pushed, decays, b_block, c_block = block
        running = jnp.cumsum(decays, axis=0)
        across = running.T
        spread = across[:, :, None] - across[:, None, :]
        kept = jnp.where(causal[None], jnp.exp(jnp.where(causal[None], spread, 0.0)), 0.0)
        scores = jnp.dot(c_block, b_block.T, precision=lax.Precision.HIGHEST)
        weighted = kept * scores[None]
        within = jnp.einsum("hts,shp->thp", weighted, pushed, precision=lax.Precision.HIGHEST)
        carried = (
            jnp.einsum("tn,hpn->thp", c_block, memory, precision=lax.Precision.HIGHEST)
            * jnp.exp(running)[:, :, None]
        )
        output = within + carried + skip_gain[None, :, None] * plain
        tail_decay = jnp.exp(running[-1][None, :] - running)
        memory = jnp.exp(running[-1])[:, None, None] * memory + jnp.einsum(
            "sh,shp,sn->hpn", tail_decay, pushed, b_block, precision=lax.Precision.HIGHEST
        )
        return (memory, output.reshape(GROUP, width))

    final_state, outputs = lax.scan(
        jax.checkpoint(advance),
        start_state,
        (
            gated.reshape(blocks, GROUP, heads, head_dim),
            driven.reshape(blocks, GROUP, heads, head_dim),
            log_decay.reshape(blocks, GROUP, heads),
            b_proj.reshape(blocks, GROUP, b_proj.shape[1]),
            c_proj.reshape(blocks, GROUP, c_proj.shape[1]),
        ),
    )
    return (outputs.reshape(length, width), final_state)


def combine(earlier, later):
    return (earlier[0] * later[0], later[0][:, :, None, None] * earlier[1] + later[1])


def body(
    tokens, out_grad, in_weight, dt_weight, bc_weight, out_weight, decay_rate, dt_bias, skip_gain
):
    seq_count = lax.axis_size("seq")
    tok_rows = tokens.shape[0]
    feat_cols = tokens.shape[1]
    width = in_weight.shape[1]
    heads = dt_weight.shape[1]
    head_dim = width // heads
    front = width + heads
    grad_scale = (tok_rows * seq_count) ** (-0.5)
    own_rows = jnp.stack([tokens, out_grad])
    gathered = lax.all_gather(own_rows, "chan", axis=2, tiled=True)
    inputs_all = jnp.stack([gathered[0], gathered[0, ::-1]])
    every_gradient = jnp.stack([gathered[1], gathered[1, ::-1]])
    packed = jnp.concatenate([in_weight, dt_weight, bc_weight, out_weight.T], 1)
    full_weights = lax.all_gather(packed, "seq", axis=0, tiled=True)
    primary_weight = full_weights[:, :front]
    bc_full = full_weights[:, front : front + 2 * STATE]
    reverse_direction_weight = full_weights[:, front + 2 * STATE :]
    projected = jnp.einsum(
        "euq,qn->eun",
        inputs_all,
        full_weights[:, : front + 2 * STATE],
        preferred_element_type=jnp.float32,
    )
    preact = projected[..., :width]
    dt_pre = projected[..., width:front] + dt_bias[:, None, :]
    bc_proj = projected[..., front:]
    gated = jax.nn.silu(preact)
    step_size = jax.nn.softplus(dt_pre)
    output_adjoint = jnp.einsum(
        "nah,hm->nam", every_gradient, reverse_direction_weight, preferred_element_type=jnp.float32
    )
    log_decay = -decay_rate[:, None, :] * step_size
    running = jnp.cumsum(log_decay, axis=1)
    total_decay = running[:, -1]
    driven = gated.reshape(2, tok_rows, heads, head_dim) * step_size[..., None]
    pushed_sum = jnp.einsum(
        "slh,slhp,sln->shpn",
        jnp.exp(total_decay[:, None, :] - running),
        driven,
        bc_proj[..., :STATE],
        precision=lax.Precision.HIGHEST,
    )
    pulled_sum = jnp.einsum(
        "slh,slhp,sln->shpn",
        jnp.exp(running),
        output_adjoint.reshape(2, tok_rows, heads, head_dim),
        bc_proj[..., STATE:],
        precision=lax.Precision.HIGHEST,
    )
    block_decay = jnp.exp(total_decay)
    identity = (jnp.ones_like(block_decay), jnp.zeros_like(pushed_sum))
    upward = carried_in(
        (block_decay, jnp.stack([pushed_sum[0], pulled_sum[1]])), "seq", combine, identity, False
    )[1]
    downward = carried_in(
        (block_decay, jnp.stack([pulled_sum[0], pushed_sum[1]])), "seq", combine, identity, True
    )[1]
    start_states = jnp.stack([upward[0], downward[1]])
    end_cots = jnp.stack([downward[0], upward[1]])

    def local_core(gated_in, step_in, bc_in, rate_in, gain_in, start_in):
        return ssd_core(
            gated_in, step_in, bc_in[:, :STATE], bc_in[:, STATE:], rate_in, gain_in, start_in
        )

    batched = jax.vmap(local_core, in_axes=(0, 0, 0, 0, None, 0))

    def pinned(gated_in, step_in, bc_in, rate_in, gain_in):
        return batched(gated_in, step_in, bc_in, rate_in, gain_in, start_states)

    (mixed, finals), pullback = jax.vjp(pinned, gated, step_size, bc_proj, decay_rate, skip_gain)
    d_gated, d_step, d_bc, d_rate, d_skip = pullback((output_adjoint, end_cots))
    sig_pre = jax.nn.sigmoid(preact)
    d_pre = d_gated * sig_pre * (1.0 + preact * (1.0 - sig_pre))
    d_z = d_step * jax.nn.sigmoid(dt_pre)
    leading_gradient = jnp.concatenate([d_pre, d_z], 2).astype(jnp.bfloat16)
    partial_grad = jnp.einsum(
        "pqx,ux->pqu", leading_gradient, primary_weight, preferred_element_type=jnp.float32
    )
    coupling_grad_applied = lax.psum(d_bc, "chan")
    coupling_rows = lax.dynamic_slice_in_dim(
        bc_full, lax.axis_index("chan") * feat_cols, feat_cols, 0
    ).astype(jnp.float32)
    coupling_section = jnp.einsum(
        "pqx,ux->pqu", coupling_grad_applied, coupling_rows, precision=lax.Precision.HIGHEST
    )
    folded = partial_grad[0] + partial_grad[1, ::-1]
    result_grad = lax.psum_scatter(folded, "chan", scatter_dimension=1, tiled=True)
    result_grad = result_grad + coupling_section[0] + coupling_section[1, ::-1]
    tokens_grad = result_grad.astype(jnp.bfloat16)
    blended_lower_half = mixed.astype(jnp.bfloat16)
    initial_section = jnp.einsum(
        "taz,tao->zo", inputs_all, leading_gradient, preferred_element_type=jnp.float32
    )
    second_part = jnp.einsum(
        "taz,tao->zo",
        inputs_all.astype(jnp.float32),
        coupling_grad_applied,
        precision=lax.Precision.HIGHEST,
    )
    final_section = jnp.einsum(
        "taz,tao->zo", every_gradient, blended_lower_half, preferred_element_type=jnp.float32
    )
    summed = lax.psum_scatter(
        grad_scale * jnp.concatenate([initial_section, second_part, final_section], 1),
        "seq",
        scatter_dimension=0,
        tiled=True,
    )
    in_weight_grad = summed[:, :width]
    dt_weight_grad = summed[:, width:front]
    bc_weight_grad = summed[:, front : front + 2 * STATE]
    out_weight_grad = summed[:, front + 2 * STATE :].T
    rate_grad, bias_grad, skip_grad = lax.psum(
        (grad_scale * d_rate * decay_rate, grad_scale * jnp.sum(d_z, axis=1), grad_scale * d_skip),
        "seq",
    )
    return (
        tokens_grad,
        in_weight_grad,
        dt_weight_grad,
        bc_weight_grad,
        out_weight_grad,
        rate_grad,
        bias_grad,
        skip_grad,
    )


def solution(mesh):
    in_specs = (
        P("seq", "chan"),
        P("seq", "chan"),
        P("seq", "chan"),
        P("seq", "chan"),
        P("seq", None),
        P("chan", "seq"),
        P(None, "chan"),
        P(None, "chan"),
        P("chan"),
    )
    out_specs = (
        P("seq", "chan"),
        P("seq", "chan"),
        P("seq", "chan"),
        P("seq", None),
        P("chan", "seq"),
        P(None, "chan"),
        P(None, "chan"),
        P("chan"),
    )
    return jax.shard_map(body, mesh=mesh, in_specs=in_specs, out_specs=out_specs, check_vma=False)
```

profile of v0, /device:TPU:0, one launch (start us, length us, event | category | flops | bytes accessed | tf_op | source)
XLA Modules:
  0.0 409.8 jit_solution(13004082430101732880)
XLA Ops:
  8.0 1.5 concatenate.10
  10.6 9.9 %all_gather.24 = bf16[2,256,512]{2,1,0:T(8,128)(2,1)S(1)} all-gather(bf16[2,256,256]{2,1,0:T(8,128)(2,1)S(1)} %pad_maximum_fusion.11), channel_id=1, replica_groups=mesh['seq'=16,'chan'=2] {'chan'}, dimensions={2}, use_global_device_ids=true | all-gather | bytes 786432 | tf_op jit(solution)/shard_map/all_gather | solution.py:88
  20.9 2.6 rev.19
  23.5 28.9 %all-gather.7.cloned.1.call-done = bf16[512,1160]{1,0:T(8,128)(2,1)} async-done(((bf16[32,1160]{1,0:T(8,128)(2,1)}), bf16[512,1160]{1,0:T(8,128)(2,1)}) %all-gather.7.cloned.1.call-update) | async-done | bytes 1187856 | tf_op jit(solution)/shard_map/all_gather | solution.py:92
  52.4 1.7 fusion.47
  57.1 1.8 fusion.50
  58.9 1.3 copy.96
  65.1 19.4 %all-gather = f32[32,1,8]{2,1,0:T(1,128)S(1)} all-gather(f32[2,1,8]{2,1,0:T(1,128)S(1)} %bitcast.193), channel_id=2, replica_groups=mesh['seq'=16,'chan'=2] {'seq'}, dimensions={0}, use_global_device_ids=true | all-gather | bytes 1088 | tf_op jit(solution)/shard_map/all_gather | solution.py:12
  85.2 1.7 fusion.89
  86.8 2.4 fusion.80
  89.2 48.2 %all-gather.9.cloned.1.call-done = f32[32,8,64,64]{3,2,1,0:T(8,128)} async-done(((f32[2,8,64,64]{3,2,1,0:T(8,128)}), f32[32,8,64,64]{3,2,1,0:T(8,128)}) %all-gather.9.cloned.1.call-update) | async-done | bytes 4194320 | tf_op jit(solution)/shard_map/all_gather | solution.py:12
  137.4 18.2 %while.20 = (s32[]{:T(128)}, f32[2,8,64,64]{3,2,1,0:T(8,128)S(1)}, s32[]{:T(128)}, f32[16,2,8]{2,1,0:T(2,128)S(1)}, f32[16,2,8,64,64]{4,3,2,1,0:T(8,128)}, /*index=5*/s32[]{:T(128)}, s32[]{:T(128)}) while((s32[]{:T(128)}, f32[2,8,64,64]{3,2,1,0:T(8,128)S(1)}, s32[]{:T(128)}, f32[16,2,8]{2,1,0:T(2,128)S(1)}, ...), condition=%wide.region_3.4_spmd.clone, body=%wide.region_2.3_spmd.clone.sunk | while | flops 262148 | bytes 786729 | solution.py:24
  139.8 1.2 fusion.115
  141.0 1.2 fusion.115
  144.7 1.2 fusion.115
  145.9 1.2 fusion.115
  150.8 1.2 fusion.115
  152.0 1.2 fusion.115
  153.2 1.2 fusion.115
  156.4 56.4 %all-gather.11.cloned.1.call-done = f32[32,8,64,64]{3,2,1,0:T(8,128)} async-done(((f32[2,8,64,64]{3,2,1,0:T(8,128)}), f32[32,8,64,64]{3,2,1,0:T(8,128)}) %all-gather.11.cloned.1.call-update) | async-done | bytes 4194320 | tf_op jit(solution)/shard_map/all_gather | solution.py:12
  212.7 8.3 %rev.21 = f32[16,2,8,64,64]{4,3,2,1,0:T(8,128)} reverse(f32[16,2,8,64,64]{4,3,2,1,0:T(8,128)} %bitcast.180), dimensions={0} | reverse | bytes 8388608 | tf_op jit(solution)/shard_map/rev | solution.py:14
  221.0 27.7 %while.21 = (s32[]{:T(128)}, f32[2,8,64,64]{3,2,1,0:T(8,128)S(1)}, s32[]{:T(128)}, f32[16,2,8]{2,1,0:T(2,128)}, f32[16,2,8,64,64]{4,3,2,1,0:T(8,128)}, /*index=5*/s32[]{:T(128)}, s32[]{:T(128)}) while((s32[]{:T(128)}, f32[2,8,64,64]{3,2,1,0:T(8,128)S(1)}, s32[]{:T(128)}, f32[16,2,8]{2,1,0:T(2,128)}, ...), condition=%wide.region_5.6_spmd.clone, body=%wide.region_4.5_spmd.clone.sunk | while | flops 262148 | bytes 786729 | solution.py:24
  250.5 2.2 reduce-window.40
  253.1 1.6 copy.97
  254.7 2.4 fusion.95
  257.1 2.0 fusion.36
  259.4 3.1 multiply_reduce_fusion.1
  262.9 2.8 convolution_bitcast_fusion.3
  265.7 7.7 %fusion.13 = (f32[2,8,256]{2,1,0:T(8,128)S(1)}, f32[2,8,256]{2,1,0:T(8,128)S(1)}, f32[2,256,256]{2,1,0:T(8,128)}) fusion(f32[2,256,256]{2,1,0:T(8,128)} %fusion.95, f32[2,8,256]{2,1,0:T(8,128)S(1)} %add_bitcast_fusion.2, pred[256,256]{1,0:T(8,128)(4,1)} %iota_compare_fusion, f32[2,8,64,256]{3,2,1,0:T(8,128)S(1)} %bitcast.173, ...), kind=kOutput, calls=%fused_computation.19 | convolution fusion | flops 816701440 | bytes 3260416 | tf_op jit(solution)/shard_map/transpose(jvp(vmap()))/while/body/eval_jaxpr/checkpoint/hts,shp->thp/dot_general | solution.py:46
  273.5 5.0 %reduce-window.42 = f32[2,8,2,128]{3,1,2,0:T(8,128)S(1)} reduce-window(f32[2,8,2,128]{3,1,2,0:T(8,128)S(1)} %fusion.70, f32[]{:T(128)} %constant.134.clone.1), window={size=1x1x1x128 pad=0_0x0_0x0_0x0_127}, to_apply=%region_14.15 | reduce-window | flops 520192 | bytes 32772 | tf_op jit(solution)/shard_map/reduce-window.4
  279.2 6.8 %broadcast_multiply_fusion = (f32[2,256,8,64]{1,3,2,0:T(8,128)}, f32[2,256,8]{1,2,0:T(8,128)}) fusion(f32[2,256,8]{1,2,0:T(8,128)S(1)} %copy-done.25, f32[2,256,648]{1,2,0:T(8,128)} %copy-done, f32[2,8,64,256]{3,2,1,0:T(8,128)S(1)} %bitcast.174, f32[2,256,256]{2,1,0:T(8,128)} %fusion.95, f32[2,8,256]{2,1,0:T(8,128)} %copy-done.31, ...), kind=kOutput, calls=%fused_computation.81 | convolution fusion | flops 811855872 | bytes 4866048 | tf_op jit(solution)/shard_map/transpose(jvp(vmap()))/while/body/eval_jaxpr/checkpoint/hts,shp->thp/dot_general | solution.py:46
  286.7 2.2 convolution_bitcast_fusion.4
  288.9 1.7 convolution_add_fusion.1
  290.6 1.4 convolution_add_fusion
  293.8 2.0 fusion.39
  298.4 4.7 %rev.22 = f32[1,256,512]{2,1,0:T(8,128)} reverse(f32[1,256,512]{2,1,0:T(8,128)} %slice.181), dimensions={1} | reverse | bytes 1048576 | tf_op jit(solution)/shard_map/rev | solution.py:165
  303.2 2.1 fusion.49
  305.4 6.2 %fusion.27 = f32[2,256,8,64]{1,3,2,0:T(8,128)S(1)} fusion(f32[2,256,8,64]{1,3,2,0:T(8,128)S(1)} %broadcast_multiply_fusion.1, f32[2,256,256]{2,1,0:T(8,128)} %fusion.80, f32[2,8,256]{2,1,0:T(8,128)S(1)} %copy-done.29, pred[256,256]{1,0:T(8,128)(4,1)S(1)} %copy-done.30), kind=kOutput, calls=%fused_computation.33 | convolution fusion | flops 809500672 | bytes 2703360 | tf_op jit(solution)/shard_map/jvp(vmap())/while/body/eval_jaxpr/hts,shp->thp/dot_general | solution.py:46
  311.7 1.4 convolution_bitcast_fusion
  313.1 2.0 fusion.35
  315.6 1.4 convolution_bitcast_fusion.2
  317.1 2.9 maximum_multiply_fusion
  320.0 3.2 copy.121
  324.9 31.9 %all-reduce.4 = (f32[2,8]{1,0:T(2,128)}, f32[2,8]{1,0:T(2,128)}, f32[8]{0:T(128)}) all-reduce(f32[2,8]{1,0:T(2,128)S(1)} %multiply_multiply_fusion, f32[2,8]{1,0:T(2,128)S(1)} %broadcast_multiply_fusion.3, f32[8]{0:T(128)S(1)} %broadcast_multiply_fusion.4), channel_id=1, replica_groups=mesh['seq'=16,'chan'=2] {'seq'}, use_global_device_ids=true, to_apply=%region_21.22 | all-reduce | flops 40 | bytes 320 | tf_op jit(solution)/shard_map/psum | solution.py:192
  357.5 1.6 fusion.57
  359.1 39.4 %reduce-scatter.7.cloned.1.call-done = f32[32,1160]{1,0:T(8,128)} async-done(((f32[512,1160]{1,0:T(8,128)}), f32[32,1160]{1,0:T(8,128)}) %reduce-scatter.7.cloned.1.call-update) | async-done | bytes 148496
  399.9 1.6 slice_bitcast_fusion.7
  401.5 1.4 slice.187
  (205 shorter events, 61.3 us)
Async XLA Ops:
  7.2 13.7 %copy-start.34 = (f32[2,8]{1,0:T(2,128)S(1)}, f32[2,8]{1,0:T(2,128)}, u32[]{:S(2)}) copy-start(f32[2,8]{1,0:T(2,128)} %param.19) | copy-start | bytes 196
  7.2 45.2 %all-gather.7.cloned.1.call-start = ((), (), s32[]{:S(2)}) async-start(), calls=%async_computation.2 | async-start | bytes 1392640 | tf_op jit(solution)/shard_map/all_gather | solution.py:92
  9.5 127.8 %all-gather.9.cloned.1.call-start = ((), (), s32[]{:S(2)}) async-start(), calls=%async_computation.5 | async-start | bytes 8912896 | tf_op jit(solution)/shard_map/all_gather | solution.py:12
  20.5 31.9 %copy-start.5 = (bf16[1,256,512]{2,1,0:T(8,128)(2,1)}, bf16[1,256,512]{2,1,0:T(8,128)(2,1)S(1)}, u32[]{:S(2)}) copy-start(bf16[1,256,512]{2,1,0:T(8,128)(2,1)S(1)} %get-tuple-element.492) | copy-start | bytes 786436
  20.5 31.9 %copy-start.9 = (bf16[1,256,512]{2,1,0:T(8,128)(2,1)}, bf16[1,256,512]{2,1,0:T(8,128)(2,1)S(1)}, u32[]{:S(2)}) copy-start(bf16[1,256,512]{2,1,0:T(8,128)(2,1)S(1)} %get-tuple-element.491) | copy-start | bytes 786436
  20.9 31.5 %copy-start.7 = (bf16[1,256,512]{2,1,0:T(8,128)(2,1)}, bf16[1,256,512]{2,1,0:T(8,128)(2,1)S(1)}, u32[]{:S(2)}) copy-start(bf16[1,256,512]{2,1,0:T(8,128)(2,1)S(1)} %rev.18) | copy-start | bytes 786436
  20.9 33.5 %copy-start.32 = (f32[2,8]{1,0:T(2,128)}, f32[2,8]{1,0:T(2,128)S(1)}, u32[]{:S(2)}) copy-start(f32[2,8]{1,0:T(2,128)S(1)} %neg.31) | copy-start | bytes 196
  23.5 30.9 %copy-start.33 = (f32[2,8]{1,0:T(2,128)S(1)}, f32[2,8]{1,0:T(2,128)}, u32[]{:S(2)}) copy-start(f32[2,8]{1,0:T(2,128)} %param.20) | copy-start | bytes 196
  54.1 7.3 %copy-start = (f32[2,256,648]{1,2,0:T(8,128)}, f32[2,256,648]{1,2,0:T(8,128)S(1)}, u32[]{:S(2)}) copy-start(f32[2,256,648]{1,2,0:T(8,128)S(1)} %fusion.47) | copy-start | bytes 3981316
  54.5 1.4 copy-start.26
  54.5 5.7 %copy-start.24 = (f32[2,256,8]{1,2,0:T(8,128)}, f32[2,256,8]{1,2,0:T(8,128)S(1)}, u32[]{:S(2)}) copy-start(f32[2,256,8]{1,2,0:T(8,128)S(1)} %get-tuple-element.478) | copy-start | bytes 49156
  56.0 0.6 copy-start.28
  58.9 1.3 copy-start.3
  60.2 1.2 copy-start.4
  63.5 149.3 %all-gather.11.cloned.1.call-start = ((), (), s32[]{:S(2)}) async-start(), calls=%async_computation.6 | async-start | bytes 8912896 | tf_op jit(solution)/shard_map/all_gather | solution.py:12
  64.4 251.2 %all-reduce.7.cloned.1.call-start = ((), (), s32[]{:S(2)}) async-start(), calls=%async_computation.4 | async-start | bytes 524288 | tf_op jit(solution)/shard_map/psum | solution.py:158
  156.4 93.3 %copy-start.11 = (f32[1,8,64,64]{3,2,1,0:T(8,128)}, f32[1,8,64,64]{3,2,1,0:T(8,128)S(1)}, u32[]{:S(2)}) copy-start(f32[1,8,64,64]{3,2,1,0:T(8,128)S(1)} %get-tuple-element.486) | copy-start | bytes 393220
  221.0 27.8 %copy-start.19 = (f32[1,8,64,64]{3,2,1,0:T(8,128)S(1)}, f32[1,8,64,64]{3,2,1,0:T(8,128)}, u32[]{:S(2)}) copy-start(f32[1,8,64,64]{3,2,1,0:T(8,128)} %get-tuple-element.485) | copy-start | bytes 393220
  248.8 4.2 %copy-start.13 = (f32[1,8,64,64]{3,2,1,0:T(8,128)}, f32[1,8,64,64]{3,2,1,0:T(8,128)S(1)}, u32[]{:S(2)}) copy-start(f32[1,8,64,64]{3,2,1,0:T(8,128)S(1)} %get-tuple-element.484) | copy-start | bytes 393220
  253.0 12.7 %copy-start.31 = (f32[2,8,256]{2,1,0:T(8,128)}, f32[2,8,256]{2,1,0:T(8,128)S(1)}, u32[]{:S(2)}) copy-start(f32[2,8,256]{2,1,0:T(8,128)S(1)} %add_bitcast_fusion.2) | copy-start | bytes 49156
  253.0 6.4 %copy-start.16 = (f32[2,256,64]{1,2,0:T(8,128)S(1)}, f32[2,256,64]{1,2,0:T(8,128)}, u32[]{:S(2)}) copy-start(f32[2,256,64]{1,2,0:T(8,128)} %get-tuple-element.361) | copy-start | bytes 393220
  254.7 4.5 %copy-start.1 = (f32[2,8,64,64]{3,2,1,0:T(8,128)S(1)}, f32[2,8,64,64]{3,2,1,0:T(8,128)}, u32[]{:S(2)}) copy-start(f32[2,8,64,64]{3,2,1,0:T(8,128)} %pad_maximum_fusion.5) | copy-start | bytes 786436
  254.7 4.5 %copy-start.2 = (f32[2,8,64,64]{3,2,1,0:T(8,128)S(1)}, f32[2,8,64,64]{3,2,1,0:T(8,128)}, u32[]{:S(2)}) copy-start(f32[2,8,64,64]{3,2,1,0:T(8,128)} %pad_maximum_fusion.6) | copy-start | bytes 786436
  265.7 13.5 %copy-start.25 = (f32[2,256,8]{1,2,0:T(8,128)S(1)}, f32[2,256,8]{1,2,0:T(8,128)}, u32[]{:S(2)}) copy-start(f32[2,256,8]{1,2,0:T(8,128)} %copy-done.24) | copy-start | bytes 49156
  278.4 7.6 %copy-start.27 = (f32[2,8,2,128]{3,1,2,0:T(8,128)}, f32[2,8,2,128]{3,1,2,0:T(8,128)S(1)}, u32[]{:S(2)}) copy-start(f32[2,8,2,128]{3,1,2,0:T(8,128)S(1)} %reduce-window.42) | copy-start | bytes 49156
  279.1 6.9 %copy-start.36 = (f32[8]{0:T(128)S(1)}, f32[8]{0:T(128)}, u32[]{:S(2)}) copy-start(f32[8]{0:T(128)} %param.21) | copy-start | bytes 100
  286.7 3.9 copy-start.15
  292.7 64.7 %reduce-scatter.5.cloned.1.call-start = ((), (), s32[]{:S(2)}) async-start(), calls=%async_computation.3 | async-start | bytes 786432 | tf_op jit(solution)/shard_map/reduce_scatter | solution.py:166
  292.8 3.1 copy-start.21
  295.8 0.8 copy-start.22
  296.6 1.0 copy-start.17
  297.6 7.7 %copy-start.29 = (f32[2,8,256]{2,1,0:T(8,128)S(1)}, f32[2,8,256]{2,1,0:T(8,128)}, u32[]{:S(2)}) copy-start(f32[2,8,256]{2,1,0:T(8,128)} %copy-done.28) | copy-start | bytes 49156
  297.6 7.8 %copy-start.30 = (pred[256,256]{1,0:T(8,128)(4,1)S(1)}, pred[256,256]{1,0:T(8,128)(4,1)}, u32[]{:S(2)}) copy-start(pred[256,256]{1,0:T(8,128)(4,1)} %iota_compare_fusion) | copy-start | bytes 196612
  305.3 6.3 %copy-start.6 = (bf16[1,256,512]{2,1,0:T(8,128)(2,1)S(1)}, bf16[1,256,512]{2,1,0:T(8,128)(2,1)}, u32[]{:S(2)}) copy-start(bf16[1,256,512]{2,1,0:T(8,128)(2,1)} %copy-done.5) | copy-start | bytes 786436
  305.3 93.2 %reduce-scatter.7.cloned.1.call-start = ((), (), s32[]{:S(2)}) async-start(), calls=%async_computation.7 | async-start | bytes 2785280
  305.4 6.2 %copy-start.8 = (bf16[1,256,512]{2,1,0:T(8,128)(2,1)S(1)}, bf16[1,256,512]{2,1,0:T(8,128)(2,1)}, u32[]{:S(2)}) copy-start(bf16[1,256,512]{2,1,0:T(8,128)(2,1)} %copy-done.7) | copy-start | bytes 786436
  305.4 6.2 %copy-start.23 = (bf16[2,256,512]{1,2,0:T(8,128)(2,1)S(1)}, bf16[2,256,512]{1,2,0:T(8,128)(2,1)}, u32[]{:S(2)}) copy-start(bf16[2,256,512]{1,2,0:T(8,128)(2,1)} %copy-done.22) | copy-start | bytes 1572868
  311.6 1.5 copy-start.12
  311.7 1.5 copy-start.14
  311.7 1.5 copy-start.37
  311.7 3.5 copy-start.10
  311.7 3.5 copy-start.20
  323.2 0.7 copy-start.35
  323.2 33.7 %copy-start.18 = (f32[2,256,128]{1,2,0:T(8,128)S(1)}, f32[2,256,128]{1,2,0:T(8,128)}, u32[]{:S(2)}) copy-start(f32[2,256,128]{1,2,0:T(8,128)} %all-reduce.7.cloned.1.call-done) | copy-start | bytes 786436
Sparse Core Ops, SparseCore 0:
  10.9 41.4 all-gather.6
  63.6 73.7 all-gather.8
  139.6 73.1 all-gather.10
  292.8 21.4 all-reduce.6
  316.5 14.5 reduce-scatter.4
  334.7 63.8 reduce-scatter.6
where the time goes:
time: 413 us; the launch traced here: 410 us
  waiting for transfers between devices  173 us (42%)
  blocking collectives  61.3 us (15%)
  other arithmetic  60.8 us (15%)
  matrix products  50.6 us (12%)
  local copies, waits for them, and re-layouts  48.5 us (12%)
  between operations  14.7 us (4%)
    all_gather x2, waiting for transfers between devices, carried_in(): pieces = jax.tree.map(lambda part: lax.all_gather(part, axis), value)  105 us
    unnamed x7, waiting for transfers between devices  39.5 us
    select_n x30, other arithmetic, step(): jnp.where(position < mine, new, old)  35.2 us
    psum x1, blocking collectives, body(): lax.psum((grad_scale * d_rate * decay_rate, grad_scale * jnp.sum(d_z, axi...  31.9 us
    all_gather x1, waiting for transfers between devices, body(): full_weights = lax.all_gather(packed, 'seq', axis=0, tiled=True)  28.9 us
    dot_general x3, matrix products, advance(): jnp.einsum('hts,shp->thp', weighted, pushed, precision=lax.Precision.HIGH...  20.8 us
    all_gather x1, blocking collectives, carried_in(): pieces = jax.tree.map(lambda part: lax.all_gather(part, axis), value)  19.4 us
    another operation x10, other arithmetic  10.6 us
  transfers between devices with their start and end apart: 6, of which 4 were waited for; matrix products, arithmetic and copies ran while one was open for 15% of the time, Pallas kernels for 0%

commit v1 on v0

v1 whole, which is shorter than its diff:
```python
import functools

import jax
import jax.numpy as jnp
from jax import lax
from jax.experimental import pallas as pl
from jax.experimental.pallas import tpu as pltpu
from jax.sharding import PartitionSpec as P

LANES = 128
F32, BF16 = jnp.float32, jnp.bfloat16
NN = (((1,), (0,)), ((), ()))
NT = (((1,), (1,)), ((), ()))
TN = (((0,), (0,)), ((), ()))


def dot(a, b, dims=NN):
    return lax.dot_general(a, b, dims, preferred_element_type=F32)


def dot32(a, b, dims=NN):
    return lax.dot_general(a, b, dims, precision=lax.Precision.HIGHEST, preferred_element_type=F32)


def halves(a):
    high = a.astype(BF16)
    return high, (a - high.astype(F32)).astype(BF16)


def dot3(a, b, dims=NN):
    return dot(a[0], b[0], dims) + (dot(a[0], b[1], dims) + dot(a[1], b[0], dims))


def kernel(
    sizes, own_ref, w_ref, vec_ref,
    tg_ref, iw_ref, dw_ref, bw_ref, ow_ref, small_ref,
    ubuf, wbuf, st, rs, po, cin, lg, gbuf, grecv, dbc_own, dbc_recv, sm, acc, sbuf, rbuf,
    u_send, u_recv, w_send, w_recv, a_send, a_recv, l_send, l_recv, b_send, b_recv,
    g_send, g_recv, d_send, d_recv, s_send, s_recv, r_send, r_recv,
):
    n, nc, T, cols, rows, width, heads, state, scale = sizes
    nb = n.bit_length() - 1
    head = width // heads
    front = width + LANES
    me, mc = lax.axis_index("seq"), lax.axis_index("chan")

    def flip(bit):
        return (1 << bit) * (1 - 2 * ((me // (1 << bit)) % 2))

    def flips(bits, subset):
        total = me
        for place, bit in enumerate(bits):
            if (subset >> place) & 1:
                total = total + flip(bit)
        return total

    def copy(src, dst, ssem, rsem, seq=None, chan=None):
        return pltpu.make_async_remote_copy(
            src_ref=src, dst_ref=dst, send_sem=ssem, recv_sem=rsem,
            device_id=(me if seq is None else seq, mc if chan is None else chan),
            device_id_type=pl.DeviceIdType.MESH,
        )

    barrier = pltpu.get_barrier_semaphore()
    for d in range(1, n):
        pl.semaphore_signal(barrier, inc=1, device_id=(lax.rem(me + d, n), mc), device_id_type=pl.DeviceIdType.MESH)
    for d in range(1, nc):
        pl.semaphore_signal(barrier, inc=1, device_id=(me, lax.rem(mc + d, nc)), device_id_type=pl.DeviceIdType.MESH)
    pl.semaphore_wait(barrier, n - 1 + nc - 1)

    u_copies = []
    for d in range(1, nc):
        c = copy(own_ref, ubuf.at[mc], u_send.at[d - 1], u_recv.at[d - 1], chan=lax.rem(mc + d, nc))
        c.start()
        u_copies.append(c)
    order = list(range(nb - 1, -1, -1))
    w_copies = []
    for i, bit in enumerate(order):
        for m in range(1 << i):
            number = (1 << i) - 1 + m
            block = flips(order[:i], m)
            if m:
                top = m.bit_length() - 1
                if top == i - 1:
                    w_copies[(1 << top) - 1 + (m - (1 << top))].wait_recv()
            c = copy(
                w_ref if m == 0 else wbuf.at[block], wbuf.at[block],
                w_send.at[number], w_recv.at[number], seq=me + flip(bit),
            )
            c.start()
            w_copies.append(c)
    ubuf[mc] = own_ref[...]
    wbuf[me] = w_ref[...]
    for c in u_copies:
        c.wait_recv()
    for c in w_copies[(1 << (nb - 1)) - 1 :]:
        c.wait_recv()

    w_all = wbuf[...].reshape(n * rows, 2 * width + 2 * LANES)
    proj = jnp.zeros((T, front + LANES), F32)
    q = jnp.zeros((T, width), F32)
    for c in range(nc):
        part = w_all[c * cols : (c + 1) * cols]
        proj = proj + dot(ubuf[c, 0], part[:, : front + LANES])
        q = q + dot(ubuf[c, 1], part[:, front + LANES :])
    pre, z, bc = proj[:, :width], proj[:, width:front], proj[:, front:]
    b_in, c_in = bc[:, :state], bc[:, state:]
    sig = 1.0 / (1.0 + jnp.exp(-pre))
    gated = pre * sig
    slope = sig * (1.0 + pre * (1.0 - sig))
    lane_head = lax.broadcasted_iota(jnp.int32, (LANES, width), 1) // head
    expand = (lane_head == lax.broadcasted_iota(jnp.int32, (LANES, width), 0)).astype(F32)
    row_i = lax.broadcasted_iota(jnp.int32, (T, T), 0)
    col_i = lax.broadcasted_iota(jnp.int32, (T, T), 1)
    lower, upper = row_i >= col_i, row_i <= col_i
    masks = (lower, upper)
    vec = vec_ref[...]
    rates = [vec[r : r + 1] for r in range(2)]
    skip = dot32(vec[4:5] + jnp.zeros((8, LANES), F32), expand)[0:1]
    b_h, c_h, q_h = halves(b_in), halves(c_in), halves(q)

    steps, zs, runs, totals, xs, e_run, e_tail = [], [], [], [], [], [], []
    pushes, pulls = [], []
    for r in range(2):
        zr = z + vec[2 + r : 3 + r]
        step = jnp.maximum(zr, 0.0) + jnp.log1p(jnp.exp(-jnp.abs(zr)))
        decay = -rates[r] * step
        run = dot32(masks[r].astype(F32), decay)
        total = run[T - 1 : T] if r == 0 else run[0:1]
        er = dot32(jnp.exp(run), expand)
        et = dot32(jnp.exp(total - run), expand)
        x = gated * dot32(step, expand)
        pushes.append(dot3(b_h, halves(et * x), TN))
        pulls.append(dot3(c_h, halves(er * q), TN))
        for held, value in ((steps, step), (zs, zr), (runs, run), (totals, total), (xs, x), (e_run, er), (e_tail, et)):
            held.append(value)
    per = 4 * state // n
    stacked = jnp.concatenate([pushes[0], pulls[1], pulls[0], pushes[1]], 0)
    st[...] = stacked.reshape(n, per, width).astype(st.dtype)
    lg[me] = jnp.concatenate([totals[0], totals[1], jnp.zeros((6, LANES), F32)], 0)
    rs[me] = st[me]
    a_copies = []
    for d in range(1, n):
        to = lax.rem(me + d, n)
        c = copy(lg.at[me], lg.at[me], l_send.at[d - 1], l_recv.at[d - 1], seq=to)
        c.start()
        e = copy(st.at[to], rs.at[me], a_send.at[d - 1], a_recv.at[d - 1], seq=to)
        e.start()
        a_copies += [c, e]

    score = dot3(c_h, b_h, NT)
    run_rows = [runs[r].T for r in range(2)]
    xh = [halves(xs[r]) for r in range(2)]
    outer = jnp.zeros((T, T), F32)
    within = [[], []]
    back = [[], []]

    def inside(r, outer):
        for j in range(heads):
            lanes = slice(j * head, (j + 1) * head)
            spread = runs[r][:, j : j + 1] - run_rows[r][j : j + 1, :]
            kept = jnp.where(masks[r], jnp.exp(jnp.where(masks[r], spread, 0.0)), 0.0)
            weighted = halves(kept * score)
            qj = (q_h[0][:, lanes], q_h[1][:, lanes])
            xj = (xh[r][0][:, lanes], xh[r][1][:, lanes])
            within[r].append(dot3(weighted, xj))
            back[r].append(dot3(weighted, qj, TN))
            outer = outer + kept * dot3(qj, xj, NT)
        return outer

    outer = inside(0, outer)

    for c in a_copies:
        c.wait_recv()
    decays = jnp.exp(dot32(lg[...].reshape(n * 8, LANES), expand)).reshape(n, 8, width)
    down = me // (n // 2)
    way = ((me * per) // state % 2).astype(F32)
    lane_dec = decays[:, 0:1] * (1.0 - way) + decays[:, 1:2] * way
    down_f = down.astype(F32)
    running = jnp.zeros((per, width), F32)
    for s in range(n):
        i = s * (1 - down) + (n - 1 - s) * down
        po[i] = running.astype(po.dtype)
        factor = lane_dec[s] * (1.0 - down_f) + lane_dec[n - 1 - s] * down_f
        running = factor * running + rs[i].astype(F32)
    cin[me] = po[me]
    b_copies = []
    for d in range(1, n):
        to = lax.rem(me + d, n)
        c = copy(po.at[to], cin.at[me], b_send.at[d - 1], b_recv.at[d - 1], seq=to)
        c.start()
        b_copies.append(c)

    outer = inside(1, outer)
    for c in b_copies:
        c.wait_recv()
    carried_all = cin[...].astype(F32).reshape(4, state, width)
    starts = (carried_all[0], carried_all[3])
    ends = (carried_all[2], carried_all[1])

    outer_h = halves(outer)
    d_c = dot3(outer_h, b_h)
    d_b = dot3(outer_h, c_h, TN)
    d_fronts, lows, small_rows = [], [], []
    bias_rows = []
    d_skip = dot32(jnp.sum(q * gated, axis=0, keepdims=True) + jnp.zeros((8, width), F32), expand, NT)[0:1] * 2.0
    for r in range(2):
        s_h, e_h = halves(starts[r]), halves(ends[r])
        y = jnp.concatenate(within[r], 1) + e_run[r] * dot3(c_h, s_h)
        tail_dx = e_tail[r] * dot3(b_h, e_h)
        dx = jnp.concatenate(back[r], 1) + tail_dx
        d_c = d_c + dot3(halves(e_run[r] * q), s_h, NT)
        d_b = d_b + dot3(halves(e_tail[r] * xs[r]), e_h, NT)
        mixed = y + skip * gated
        lows.append(mixed.astype(BF16))
        d_run = dot32(q * y - xs[r] * dx, expand, NT)
        ends_sum = jnp.sum(xs[r] * tail_dx, axis=0, keepdims=True)
        keep_row = e_run[r][T - 1 : T] if r == 0 else e_run[r][0:1]
        ends_sum = ends_sum + jnp.sum(ends[r] * starts[r] * keep_row, axis=0, keepdims=True)
        d_total = dot32(ends_sum + jnp.zeros((8, width), F32), expand, NT)[0:1]
        d_decay = dot32(masks[1 - r].astype(F32), d_run) + d_total
        step_wide = dot32(steps[r], expand)
        d_gated = skip * q + step_wide * dx
        d_step = dot32(gated * dx, expand, NT) - rates[r] * d_decay
        d_z = d_step / (1.0 + jnp.exp(-zs[r]))
        small_rows.append(-rates[r] * jnp.sum(steps[r] * d_decay, axis=0, keepdims=True))
        bias_rows.append(jnp.sum(d_z, axis=0, keepdims=True))
        d_fronts.append(jnp.concatenate([d_gated * slope, d_z], 1).astype(BF16))
    d_bc = jnp.concatenate([d_b, d_c], 1)
    dbc_own[...] = d_bc
    sm[me] = scale * jnp.concatenate(small_rows + bias_rows + [d_skip, jnp.zeros((3, LANES), F32)], 0)
    d_copies = []
    for d in range(1, nc):
        c = copy(dbc_own, dbc_recv.at[d - 1], d_send.at[d - 1], d_recv.at[d - 1], chan=lax.rem(mc + d, nc))
        c.start()
        d_copies.append(c)
    s_copies = []
    for d in range(1, n):
        c = copy(sm.at[me], sm.at[me], s_send.at[d - 1], s_recv.at[d - 1], seq=lax.rem(me + d, n))
        c.start()
        s_copies.append(c)

    dbc_h = halves(d_bc)
    w_all = wbuf[...].reshape(n * rows, 2 * width + 2 * LANES)
    for c in range(nc):
        part = w_all[c * cols : (c + 1) * cols]
        lead, maps = part[:, :front], part[:, front : front + LANES]
        g = dot(d_fronts[0], lead, NT) + dot(d_fronts[1], lead, NT)
        gbuf[c] = g + (dot(dbc_h[0], maps, NT) + dot(dbc_h[1], maps, NT))
    g_copies = []
    for d in range(1, nc):
        to = lax.rem(mc + d, nc)
        c = copy(gbuf.at[to], grecv.at[d - 1], g_send.at[d - 1], g_recv.at[d - 1], chan=to)
        c.start()
        g_copies.append(c)

    for c in d_copies:
        c.wait_recv()
    for d in range(1, nc):
        d_bc = d_bc + dbc_recv[d - 1]
    dbc_h = halves(d_bc)
    per_chan = cols // rows
    for c in range(nc):
        u, cot = ubuf[c, 0], ubuf[c, 1]
        lead = dot(u, d_fronts[0], TN) + dot(u, d_fronts[1], TN)
        maps = dot(u, dbc_h[0], TN) + dot(u, dbc_h[1], TN)
        outs = dot(cot, lows[0], TN) + dot(cot, lows[1], TN)
        packed = scale * jnp.concatenate([lead, maps, outs], 1)
        acc[c * per_chan : (c + 1) * per_chan] = packed.reshape(per_chan, rows, 2 * width + 2 * LANES)
    number = 0
    r_copies = []
    for bit in range(nb):
        higher = list(range(bit + 1, nb))
        first = number
        for m in range(1 << len(higher)):
            block = flips(higher, m) + flip(bit)
            sbuf[number] = acc[block].astype(BF16)
            c = copy(sbuf.at[number], rbuf.at[number], r_send.at[number], r_recv.at[number], seq=me + flip(bit))
            c.start()
            r_copies.append(c)
            number += 1
        for m in range(1 << len(higher)):
            r_copies[first + m].wait_recv()
            block = flips(higher, m)
            acc[block] = acc[block] + rbuf[first + m].astype(F32)
    done = acc[me]
    iw_ref[...] = done[:, :width]
    dw_ref[...] = done[:, width : width + heads]
    bw_ref[...] = done[:, front : front + LANES]
    ow_ref[...] = done[:, front + LANES :]
    for c in g_copies:
        c.wait_recv()
    g = gbuf[mc]
    for d in range(1, nc):
        g = g + grecv[d - 1]
    tg_ref[...] = g.astype(BF16)
    for c in s_copies:
        c.wait_recv()
    total = sm[0]
    for i in range(1, n):
        total = total + sm[i]
    small_ref[...] = total
    for c in u_copies + w_copies + a_copies + b_copies + d_copies + s_copies + g_copies + r_copies:
        c.wait_send()


def body(n, nc, tokens, out_grad, in_weight, dt_weight, bc_weight, out_weight, decay_rate, dt_bias, skip_gain):
    T, cols = tokens.shape
    rows, width = in_weight.shape
    heads = dt_weight.shape[1]
    state = bc_weight.shape[1] // 2
    scale = float(T * n) ** -0.5
    own = jnp.stack([tokens, out_grad])
    dt_wide = jnp.pad(dt_weight, ((0, 0), (0, LANES - heads)))
    packed = jnp.concatenate([in_weight, dt_wide, bc_weight, out_weight.T], 1)
    total_w = packed.shape[1]
    vec = jnp.pad(
        jnp.concatenate([decay_rate, dt_bias, skip_gain[None]], 0), ((0, 3), (0, LANES - heads))
    )
    per = 4 * state // n
    dma = pltpu.SemaphoreType.DMA
    seq_sems, chan_sems = dma((n - 1,)), dma((nc - 1,))
    vmem = pl.BlockSpec(memory_space=pltpu.VMEM)
    sizes = (n, nc, T, cols, rows, width, heads, state, scale)
    tg, iw, dw, bw, ow, small = pl.pallas_call(
        functools.partial(kernel, sizes),
        out_shape=(
            jax.ShapeDtypeStruct((T, cols), BF16),
            jax.ShapeDtypeStruct((rows, width), F32),
            jax.ShapeDtypeStruct((rows, heads), F32),
            jax.ShapeDtypeStruct((rows, 2 * state), F32),
            jax.ShapeDtypeStruct((rows, width), F32),
            jax.ShapeDtypeStruct((8, LANES), F32),
        ),
        in_specs=[vmem] * 3,
        out_specs=(vmem,) * 6,
        scratch_shapes=[
            pltpu.VMEM((nc, 2, T, cols), BF16),
            pltpu.VMEM((n, rows, total_w), BF16),
            pltpu.VMEM((n, per, width), F32),
            pltpu.VMEM((n, per, width), F32),
            pltpu.VMEM((n, per, width), F32),
            pltpu.VMEM((n, per, width), F32),
            pltpu.VMEM((n, 8, LANES), F32),
            pltpu.VMEM((nc, T, cols), F32),
            pltpu.VMEM((nc - 1, T, cols), F32),
            pltpu.VMEM((T, 2 * state), F32),
            pltpu.VMEM((nc - 1, T, 2 * state), F32),
            pltpu.VMEM((n, 8, LANES), F32),
            pltpu.VMEM((n, rows, total_w), F32),
            pltpu.VMEM((n - 1, rows, total_w), BF16),
            pltpu.VMEM((n - 1, rows, total_w), BF16),
            chan_sems, chan_sems, seq_sems, seq_sems, seq_sems, seq_sems, seq_sems, seq_sems, seq_sems, seq_sems,
            chan_sems, chan_sems, chan_sems, chan_sems, seq_sems, seq_sems, seq_sems, seq_sems,
        ],
        compiler_params=pltpu.CompilerParams(
            collective_id=0, has_side_effects=True, vmem_limit_bytes=48 * 1024 * 1024
        ),
        cost_estimate=pl.CostEstimate(flops=4 * 10**9, bytes_accessed=4 * 10**6, transcendentals=10**6),
    )(own, packed, vec)
    return (
        tg, iw, dw, bw, ow.T, small[0:2, :heads], small[2:4, :heads], small[4, :heads],
    )


def solution(mesh):
    in_specs = (
        P("seq", "chan"),
        P("seq", "chan"),
        P("seq", "chan"),
        P("seq", "chan"),
        P("seq", None),
        P("chan", "seq"),
        P(None, "chan"),
        P(None, "chan"),
        P("chan"),
    )
    out_specs = (
        P("seq", "chan"),
        P("seq", "chan"),
        P("seq", "chan"),
        P("seq", None),
        P("chan", "seq"),
        P(None, "chan"),
        P(None, "chan"),
        P("chan"),
    )
    local = functools.partial(body, mesh.shape["seq"], mesh.shape["chan"])
    return jax.shard_map(local, mesh=mesh, in_specs=in_specs, out_specs=out_specs, check_vma=False)
```

time: 413 us -> 102 us (0.25)
  waiting for transfers between devices: 173 us -> 0 us
  Pallas kernels: 0 us -> 93.8 us
  blocking collectives: 61.3 us -> 0 us
  other arithmetic: 60.8 us -> 2.49 us
  matrix products: 50.6 us -> 0 us
  local copies, waits for them, and re-layouts: 48.5 us -> 5.03 us
  between operations: 14.7 us -> 0.66 us
    all_gather x3 -> x0, waiting for transfers between devices: 133 us -> none  [the longest x2 105 us: carried_in(): pieces = jax.tree.map(lambda part: lax.all_gather(part, axis), value)]
    pallas_call x0 -> x1, Pallas kernels: none -> 93.8 us  [body(): pl.pallas_call(functools.partial(kernel, sizes), out_shape=(jax.ShapeDtyp...]
    dot_general x21 -> x0, matrix products: 50.6 us -> none  [the longest x3 20.8 us: advance(): jnp.einsum('hts,shp->thp', weighted, pushed, precision=lax.Precision.HIGH...]
    unnamed x7 -> x0, waiting for transfers between devices: 39.5 us -> none
    select_n x30 -> x0, other arithmetic: 35.2 us -> none  [step(): jnp.where(position < mine, new, old)]
    psum x1 -> x0, blocking collectives: 31.9 us -> none  [body(): lax.psum((grad_scale * d_rate * decay_rate, grad_scale * jnp.sum(d_z, axi...]
    all_gather x2 -> x0, blocking collectives: 29.4 us -> none  [the longest x1 19.4 us: carried_in(): pieces = jax.tree.map(lambda part: lax.all_gather(part, axis), value)]
    rev x6 -> x0, local copies, waits for them, and re-layouts: 16.7 us -> none  [the longest x2 8.85 us: carried_in(): pieces = jax.tree.map(lambda part: part[::-1], pieces)]
  transfers between devices with their start and end apart: 6 -> 0, of which waited for: 4 -> 0; matrix products, arithmetic and copies ran while one was open for 15% -> 0% of each run, Pallas kernels for 0% -> 0%
where the time goes in v1:
time: 102 us
  Pallas kernels  93.8 us (92%)
  local copies, waits for them, and re-layouts  5.03 us (5%)
  other arithmetic  2.49 us (2%)
    pallas_call x1, Pallas kernels, body(): pl.pallas_call(functools.partial(kernel, sizes), out_shape=(jax.ShapeDtyp...  93.8 us
    unnamed x8, local copies, waits for them, and re-layouts  3.95 us

profile of v1, /device:TPU:0, one launch (start us, length us, event | category | flops | bytes accessed | tf_op | source)
XLA Modules:
  0.0 101.9 jit_solution(10892522839670136979)
XLA Ops:
  0.6 0.0 copy-start
  0.6 0.8 select_maximum_fusion.vec_ref
  1.4 0.8 copy.17
  2.2 0.8 fusion.4.w_ref
  3.0 0.0 copy-done
  3.0 0.9 pad_maximum_fusion.own_ref
  3.9 93.8 %shard_map.152 = (bf16[256,256]{1,0:T(8,128)(2,1)S(1)}, f32[32,512]{1,0:T(8,128)S(1)}, f32[32,8]{1,0:T(8,128)S(1)}, f32[32,128]{1,0:T(8,128)S(1)}, f32[32,512]{1,0:T(8,128)S(1)}, /*index=5*/f32[8,128]{1,0:T(8,128)S(1)}) custom-call(bf16[2,256,256]{2,1,0:T(8,128)(2,1)S(1)} %pad_maximum_fusion.own_ref, bf16[32,1280]{1,0:T(8,128)(2,1)S(1)} %fusion.4.w_ref, ...), custom_call_target="tpu_custom_call" | custom-call | flops 4000000000 | bytes 4000000 | tf_op jit(solution)/shard_map/pallas_call | solution.py:325
  97.7 0.5 slice_bitcast_fusion
  98.2 0.6 fusion.5
  98.8 0.7 copy.18
  99.4 0.7 copy.23
  100.1 0.6 copy.24
  100.7 0.6 copy.25
  101.3 0.6 copy.26
Async XLA Ops:
  0.6 2.3 %copy-start = (bf16[256,256]{1,0:T(8,128)(2,1)S(1)}, bf16[256,256]{1,0:T(8,128)(2,1)}, u32[]{:S(2)}) copy-start(bf16[256,256]{1,0:T(8,128)(2,1)} %param.10) | copy-start | bytes 393220

commit v2 on v1

--- a/solution.py
+++ b/solution.py
@@ -32,11 +32,12 @@
 
 
 def kernel(
-    sizes, own_ref, w_ref, vec_ref,
+    sizes, tok_ref, og_ref, inw_ref, dtw_ref, bcw_ref, outw_ref, rate_ref, bias_ref, gain_ref,
     tg_ref, iw_ref, dw_ref, bw_ref, ow_ref, small_ref,
-    ubuf, wbuf, st, rs, po, cin, lg, gbuf, grecv, dbc_own, dbc_recv, sm, acc, sbuf, rbuf,
+    ubuf, wbuf, st, rs, po, cin, lg, gbuf, grecv, dbc_own, dbc_recv, sm, vec_ref,
+    acc_o, acc_l, first_o, first_l, sbuf_o, sbuf_l, rbuf_o, rbuf_l,
     u_send, u_recv, w_send, w_recv, a_send, a_recv, l_send, l_recv, b_send, b_recv,
-    g_send, g_recv, d_send, d_recv, s_send, s_recv, r_send, r_recv,
+    g_send, g_recv, d_send, d_recv, s_send, s_recv, o_send, o_recv, r_send, r_recv,
 ):
     n, nc, T, cols, rows, width, heads, state, scale = sizes
     nb = n.bit_length() - 1
@@ -61,6 +62,21 @@
             device_id_type=pl.DeviceIdType.MESH,
         )
 
+    ubuf[mc, 0] = tok_ref[...]
+    ubuf[mc, 1] = og_ref[...]
+    eye = (
+        lax.broadcasted_iota(jnp.int32, (width, width), 0) == lax.broadcasted_iota(jnp.int32, (width, width), 1)
+    ).astype(BF16)
+    wbuf[me, :, :width] = inw_ref[...]
+    wbuf[me, :, width:front] = jnp.zeros((rows, LANES), BF16)
+    wbuf[me, :, width : width + heads] = dtw_ref[...]
+    wbuf[me, :, front : front + LANES] = bcw_ref[...]
+    wbuf[me, :, front + LANES :] = dot(outw_ref[...], eye, TN).astype(BF16)
+    vec_ref[...] = jnp.zeros((8, LANES), F32)
+    vec_ref[0:2, :heads] = rate_ref[...]
+    vec_ref[2:4, :heads] = bias_ref[...]
+    vec_ref[4:5, :heads] = gain_ref[...]
+
     barrier = pltpu.get_barrier_semaphore()
     for d in range(1, n):
         pl.semaphore_signal(barrier, inc=1, device_id=(lax.rem(me + d, n), mc), device_id_type=pl.DeviceIdType.MESH)
@@ -68,33 +84,30 @@
         pl.semaphore_signal(barrier, inc=1, device_id=(me, lax.rem(mc + d, nc)), device_id_type=pl.DeviceIdType.MESH)
     pl.semaphore_wait(barrier, n - 1 + nc - 1)
 
+    order = list(range(nb - 1, -1, -1))
+    w_copies = {}
+
+    def pass_on(m, after):
+        block = flips(order, m)
+        for i in range(after, nb):
+            number = (1 << i) - 1 + m
+            c = copy(wbuf.at[block], wbuf.at[block], w_send.at[number], w_recv.at[number], seq=me + flip(order[i]))
+            c.start()
+            w_copies[i, m] = c
+
+    pass_on(0, 0)
     u_copies = []
     for d in range(1, nc):
-        c = copy(own_ref, ubuf.at[mc], u_send.at[d - 1], u_recv.at[d - 1], chan=lax.rem(mc + d, nc))
+        c = copy(ubuf.at[mc], ubuf.at[mc], u_send.at[d - 1], u_recv.at[d - 1], chan=lax.rem(mc + d, nc))
         c.start()
         u_copies.append(c)
-    order = list(range(nb - 1, -1, -1))
-    w_copies = []
-    for i, bit in enumerate(order):
-        for m in range(1 << i):
-            number = (1 << i) - 1 + m
-            block = flips(order[:i], m)
-            if m:
-                top = m.bit_length() - 1
-                if top == i - 1:
-                    w_copies[(1 << top) - 1 + (m - (1 << top))].wait_recv()
-            c = copy(
-                w_ref if m == 0 else wbuf.at[block], wbuf.at[block],
-                w_send.at[number], w_recv.at[number], seq=me + flip(bit),
-            )
-            c.start()
-            w_copies.append(c)
-    ubuf[mc] = own_ref[...]
-    wbuf[me] = w_ref[...]
+    arrivals = sorted(((i, m) for i in range(nb) for m in range(1 << i)), key=lambda e: (e[1].bit_count(), e))
+    for i, m in arrivals:
+        w_copies[i, m].wait_recv()
+        pass_on(m + (1 << i), i + 1)
     for c in u_copies:
         c.wait_recv()
-    for c in w_copies[(1 << (nb - 1)) - 1 :]:
-        c.wait_recv()
+    w_copies = list(w_copies.values())
 
     w_all = wbuf[...].reshape(n * rows, 2 * width + 2 * LANES)
     proj = jnp.zeros((T, front + LANES), F32)
@@ -108,6 +121,36 @@
     sig = 1.0 / (1.0 + jnp.exp(-pre))
     gated = pre * sig
     slope = sig * (1.0 + pre * (1.0 - sig))
+    per_chan = cols // rows
+    priority = sorted(range(n // 2), key=lambda m: tuple(-((m >> p) & 1) for p in range(nb)))
+
+    def begin(acc, first, send, recv, held):
+        for m in priority:
+            block = flips(range(1, nb), m) + flip(0)
+            c = copy(acc.at[block], first.at[m], send.at[m], recv.at[m], seq=me + flip(0))
+            c.start()
+            held[0, m] = c
+
+    def advance(bit, acc, first, sbuf, rbuf, send, recv, held):
+        base = n - (n >> bit)
+        for m in (m for m in priority if m < (n >> (bit + 1))):
+            held[bit, m].wait_recv()
+            block = flips(range(bit + 1, nb), m)
+            got = first[m] if bit == 0 else rbuf[base - n // 2 + m].astype(F32)
+            value = acc[block] + got
+            if m & 1:
+                number = n - (n >> (bit + 1)) + (m >> 1)
+                slot = number - n // 2
+                sbuf[slot] = value.astype(BF16)
+                c = copy(sbuf.at[slot], rbuf.at[slot], send.at[number], recv.at[number], seq=me + flip(bit + 1))
+                c.start()
+                held[bit + 1, m >> 1] = c
+            else:
+                acc[block] = value
+
+    o_held, l_held = {}, {}
+    o_args = (acc_o, first_o, sbuf_o, rbuf_o, o_send, o_recv, o_held)
+    l_args = (acc_l, first_l, sbuf_l, rbuf_l, r_send, r_recv, l_held)
     lane_head = lax.broadcasted_iota(jnp.int32, (LANES, width), 1) // head
     expand = (lane_head == lax.broadcasted_iota(jnp.int32, (LANES, width), 0)).astype(F32)
     row_i = lax.broadcasted_iota(jnp.int32, (T, T), 0)
@@ -204,36 +247,48 @@
     d_fronts, lows, small_rows = [], [], []
     bias_rows = []
     d_skip = dot32(jnp.sum(q * gated, axis=0, keepdims=True) + jnp.zeros((8, width), F32), expand, NT)[0:1] * 2.0
+    ys, tails, dxs, s_hs, e_hs = [], [], [], [], []
     for r in range(2):
         s_h, e_h = halves(starts[r]), halves(ends[r])
         y = jnp.concatenate(within[r], 1) + e_run[r] * dot3(c_h, s_h)
-        tail_dx = e_tail[r] * dot3(b_h, e_h)
-        dx = jnp.concatenate(back[r], 1) + tail_dx
-        d_c = d_c + dot3(halves(e_run[r] * q), s_h, NT)
-        d_b = d_b + dot3(halves(e_tail[r] * xs[r]), e_h, NT)
-        mixed = y + skip * gated
-        lows.append(mixed.astype(BF16))
+        lows.append((y + skip * gated).astype(BF16))
+        ys.append(y)
+        s_hs.append(s_h)
+        e_hs.append(e_h)
+    for c in range(nc):
+        cot = ubuf[c, 1]
+        outs = scale * (dot(cot, lows[0], TN) + dot(cot, lows[1], TN))
+        acc_o[c * per_chan : (c + 1) * per_chan] = outs.reshape(per_chan, rows, width)
+    begin(acc_o, first_o, o_send, o_recv, o_held)
+    for r in range(2):
+        tail_dx = e_tail[r] * dot3(b_h, e_hs[r])
+        tails.append(tail_dx)
+        dxs.append(jnp.concatenate(back[r], 1) + tail_dx)
+        d_c = d_c + dot3(halves(e_run[r] * q), s_hs[r], NT)
+        d_b = d_b + dot3(halves(e_tail[r] * xs[r]), e_hs[r], NT)
+    d_bc = jnp.concatenate([d_b, d_c], 1)
+    dbc_own[...] = d_bc
+    d_copies = []
+    for d in range(1, nc):
+        c = copy(dbc_own, dbc_recv.at[d - 1], d_send.at[d - 1], d_recv.at[d - 1], chan=lax.rem(mc + d, nc))
+        c.start()
+        d_copies.append(c)
+    advance(0, *o_args)
+    for r in range(2):
+        y, tail_dx, dx = ys[r], tails[r], dxs[r]
         d_run = dot32(q * y - xs[r] * dx, expand, NT)
         ends_sum = jnp.sum(xs[r] * tail_dx, axis=0, keepdims=True)
         keep_row = e_run[r][T - 1 : T] if r == 0 else e_run[r][0:1]
         ends_sum = ends_sum + jnp.sum(ends[r] * starts[r] * keep_row, axis=0, keepdims=True)
         d_total = dot32(ends_sum + jnp.zeros((8, width), F32), expand, NT)[0:1]
         d_decay = dot32(masks[1 - r].astype(F32), d_run) + d_total
-        step_wide = dot32(steps[r], expand)
-        d_gated = skip * q + step_wide * dx
+        d_gated = skip * q + dot32(steps[r], expand) * dx
         d_step = dot32(gated * dx, expand, NT) - rates[r] * d_decay
         d_z = d_step / (1.0 + jnp.exp(-zs[r]))
         small_rows.append(-rates[r] * jnp.sum(steps[r] * d_decay, axis=0, keepdims=True))
         bias_rows.append(jnp.sum(d_z, axis=0, keepdims=True))
         d_fronts.append(jnp.concatenate([d_gated * slope, d_z], 1).astype(BF16))
-    d_bc = jnp.concatenate([d_b, d_c], 1)
-    dbc_own[...] = d_bc
     sm[me] = scale * jnp.concatenate(small_rows + bias_rows + [d_skip, jnp.zeros((3, LANES), F32)], 0)
-    d_copies = []
-    for d in range(1, nc):
-        c = copy(dbc_own, dbc_recv.at[d - 1], d_send.at[d - 1], d_recv.at[d - 1], chan=lax.rem(mc + d, nc))
-        c.start()
-        d_copies.append(c)
     s_copies = []
     for d in range(1, n):
         c = copy(sm.at[me], sm.at[me], s_send.at[d - 1], s_recv.at[d - 1], seq=lax.rem(me + d, n))
@@ -259,35 +314,23 @@
     for d in range(1, nc):
         d_bc = d_bc + dbc_recv[d - 1]
     dbc_h = halves(d_bc)
-    per_chan = cols // rows
     for c in range(nc):
-        u, cot = ubuf[c, 0], ubuf[c, 1]
+        u = ubuf[c, 0]
         lead = dot(u, d_fronts[0], TN) + dot(u, d_fronts[1], TN)
         maps = dot(u, dbc_h[0], TN) + dot(u, dbc_h[1], TN)
-        outs = dot(cot, lows[0], TN) + dot(cot, lows[1], TN)
-        packed = scale * jnp.concatenate([lead, maps, outs], 1)
-        acc[c * per_chan : (c + 1) * per_chan] = packed.reshape(per_chan, rows, 2 * width + 2 * LANES)
-    number = 0
-    r_copies = []
-    for bit in range(nb):
-        higher = list(range(bit + 1, nb))
-        first = number
-        for m in range(1 << len(higher)):
-            block = flips(higher, m) + flip(bit)
-            sbuf[number] = acc[block].astype(BF16)
-            c = copy(sbuf.at[number], rbuf.at[number], r_send.at[number], r_recv.at[number], seq=me + flip(bit))
-            c.start()
-            r_copies.append(c)
-            number += 1
-        for m in range(1 << len(higher)):
-            r_copies[first + m].wait_recv()
-            block = flips(higher, m)
-            acc[block] = acc[block] + rbuf[first + m].astype(F32)
-    done = acc[me]
+        packed = scale * jnp.concatenate([lead, maps], 1)
+        acc_l[c * per_chan : (c + 1) * per_chan] = packed.reshape(per_chan, rows, front + LANES)
+    begin(acc_l, first_l, r_send, r_recv, l_held)
+    for bit in range(1, nb):
+        advance(bit, *o_args)
+        advance(bit - 1, *l_args)
+    advance(nb - 1, *l_args)
+    r_copies = list(o_held.values()) + list(l_held.values())
+    done = acc_l[me]
     iw_ref[...] = done[:, :width]
     dw_ref[...] = done[:, width : width + heads]
-    bw_ref[...] = done[:, front : front + LANES]
-    ow_ref[...] = done[:, front + LANES :]
+    bw_ref[...] = done[:, front:]
+    ow_ref[...] = acc_o[me]
     for c in g_copies:
         c.wait_recv()
     g = gbuf[mc]
@@ -310,13 +353,8 @@
     heads = dt_weight.shape[1]
     state = bc_weight.shape[1] // 2
     scale = float(T * n) ** -0.5
-    own = jnp.stack([tokens, out_grad])
-    dt_wide = jnp.pad(dt_weight, ((0, 0), (0, LANES - heads)))
-    packed = jnp.concatenate([in_weight, dt_wide, bc_weight, out_weight.T], 1)
-    total_w = packed.shape[1]
-    vec = jnp.pad(
-        jnp.concatenate([decay_rate, dt_bias, skip_gain[None]], 0), ((0, 3), (0, LANES - heads))
-    )
+    total_w = 2 * width + 2 * LANES
+    lead_w = width + 2 * LANES
     per = 4 * state // n
     dma = pltpu.SemaphoreType.DMA
     seq_sems, chan_sems = dma((n - 1,)), dma((nc - 1,))
@@ -332,7 +370,7 @@
             jax.ShapeDtypeStruct((rows, width), F32),
             jax.ShapeDtypeStruct((8, LANES), F32),
         ),
-        in_specs=[vmem] * 3,
+        in_specs=[vmem] * 9,
         out_specs=(vmem,) * 6,
         scratch_shapes=[
             pltpu.VMEM((nc, 2, T, cols), BF16),
@@ -347,17 +385,26 @@
             pltpu.VMEM((T, 2 * state), F32),
             pltpu.VMEM((nc - 1, T, 2 * state), F32),
             pltpu.VMEM((n, 8, LANES), F32),
-            pltpu.VMEM((n, rows, total_w), F32),
-            pltpu.VMEM((n - 1, rows, total_w), BF16),
-            pltpu.VMEM((n - 1, rows, total_w), BF16),
+            pltpu.VMEM((8, LANES), F32),
+            pltpu.VMEM((n, rows, width), F32),
+            pltpu.VMEM((n, rows, lead_w), F32),
+            pltpu.VMEM((n // 2, rows, width), F32),
+            pltpu.VMEM((n // 2, rows, lead_w), F32),
+            pltpu.VMEM((n // 2 - 1, rows, width), BF16),
+            pltpu.VMEM((n // 2 - 1, rows, lead_w), BF16),
+            pltpu.VMEM((n // 2 - 1, rows, width), BF16),
+            pltpu.VMEM((n // 2 - 1, rows, lead_w), BF16),
             chan_sems, chan_sems, seq_sems, seq_sems, seq_sems, seq_sems, seq_sems, seq_sems, seq_sems, seq_sems,
-            chan_sems, chan_sems, chan_sems, chan_sems, seq_sems, seq_sems, seq_sems, seq_sems,
+            chan_sems, chan_sems, chan_sems, chan_sems, seq_sems, seq_sems, seq_sems, seq_sems, seq_sems, seq_sems,
         ],
         compiler_params=pltpu.CompilerParams(
             collective_id=0, has_side_effects=True, vmem_limit_bytes=48 * 1024 * 1024
         ),
         cost_estimate=pl.CostEstimate(flops=4 * 10**9, bytes_accessed=4 * 10**6, transcendentals=10**6),
-    )(own, packed, vec)
+    )(
+        tokens, out_grad, in_weight, dt_weight, bc_weight, out_weight,
+        decay_rate, dt_bias, skip_gain.reshape(1, heads),
+    )
     return (
         tg, iw, dw, bw, ow.T, small[0:2, :heads], small[2:4, :heads], small[4, :heads],
     )

time: 102 us -> 89.3 us (0.88)
  Pallas kernels: 93.8 us -> 81.4 us
  other arithmetic: 2.49 us -> 0 us
  local copies, waits for them, and re-layouts: 5.03 us -> 6.91 us
    pallas_call x1, Pallas kernels: 93.8 us -> 81.4 us  [body(): pl.pallas_call(functools.partial(kernel, sizes), out_shape=(jax.ShapeDtyp...]
    unnamed x8 -> x21, local copies, waits for them, and re-layouts: 3.95 us -> 5.83 us
    concatenate x2 -> x0, other arithmetic: 1.56 us -> none  [the longest x1 0.8 us: body(): packed = jnp.concatenate([in_weight, dt_wide, bc_weight, out_weight.T], 1)]
where the time goes in v2:
time: 89.3 us; the launch traced here: 89.1 us
  Pallas kernels  81.4 us (91%)
  local copies, waits for them, and re-layouts  6.91 us (8%)
    pallas_call x1, Pallas kernels, body(): pl.pallas_call(functools.partial(kernel, sizes), out_shape=(jax.ShapeDtyp...  81.4 us
    unnamed x21, local copies, waits for them, and re-layouts  5.83 us

profile of v2, /device:TPU:0, one launch (start us, length us, event | category | flops | bytes accessed | tf_op | source)
XLA Modules:
  0.0 89.1 jit_solution(7134806118623053038)
XLA Ops:
  0.6 0.0 copy-start
  0.6 0.8 copy.17.dtw_ref
  1.4 0.0 copy-start.2
  1.4 0.0 copy-start.3
  1.4 0.0 copy-start.4
  1.5 0.0 copy-start.5
  1.5 0.0 copy-start.6
  1.5 0.9 %copy.18.outw_ref = bf16[512,32]{1,0:T(8,128)(2,1)S(1)} copy(bf16[512,32]{0,1:T(8,128)(2,1)} %param.14) | data formatting | bytes 65536 | tf_op args[5]
  2.4 0.0 copy-done
  2.4 0.0 copy-done.2
  2.4 0.0 copy-done.3
  2.4 0.0 copy-done.4
  2.4 0.0 copy-done.5
  2.5 0.0 copy-done.6
  2.5 0.0 copy-start.1
  2.5 0.9 %copy-done.1 = bf16[256,256]{1,0:T(8,128)(2,1)S(1)} copy-done((bf16[256,256]{1,0:T(8,128)(2,1)S(1)}, bf16[256,256]{1,0:T(8,128)(2,1)}, u32[]{:S(2)}) %copy-start.1) | copy-done | bytes 131096
  3.4 81.4 %shard_map.152 = (bf16[256,256]{1,0:T(8,128)(2,1)S(1)}, f32[32,512]{1,0:T(8,128)S(1)}, f32[32,8]{1,0:T(8,128)S(1)}, f32[32,128]{1,0:T(8,128)S(1)}, f32[32,512]{1,0:T(8,128)S(1)}, /*index=5*/f32[8,128]{1,0:T(8,128)S(1)}) custom-call(bf16[256,256]{1,0:T(8,128)(2,1)S(1)} %copy-done, bf16[256,256]{1,0:T(8,128)(2,1)S(1)} %copy-done.1, ...), custom_call_target="tpu_custom_call" | custom-call | flops 4000000000 | bytes 4000000 | tf_op jit(solution)/shard_map/pallas_call | solution.py:363
  84.8 0.5 slice_bitcast_fusion
  85.3 0.6 fusion
  85.9 0.7 copy.19
  86.6 0.7 copy.24
  87.2 0.6 copy.25
  87.8 0.6 copy.26
  88.4 0.6 copy.27
Async XLA Ops:
  0.6 1.8 %copy-start = (bf16[256,256]{1,0:T(8,128)(2,1)S(1)}, bf16[256,256]{1,0:T(8,128)(2,1)}, u32[]{:S(2)}) copy-start(bf16[256,256]{1,0:T(8,128)(2,1)} %tok_ref.1) | copy-start | bytes 393220
  1.4 1.0 %copy-start.2 = (bf16[32,512]{1,0:T(8,128)(2,1)S(1)}, bf16[32,512]{1,0:T(8,128)(2,1)}, u32[]{:S(2)}) copy-start(bf16[32,512]{1,0:T(8,128)(2,1)} %inw_ref.1) | copy-start | bytes 98308
  1.4 1.0 %copy-start.3 = (bf16[32,128]{1,0:T(8,128)(2,1)S(1)}, bf16[32,128]{1,0:T(8,128)(2,1)}, u32[]{:S(2)}) copy-start(bf16[32,128]{1,0:T(8,128)(2,1)} %bcw_ref.1) | copy-start | bytes 24580
  1.4 1.0 %copy-start.4 = (f32[2,8]{1,0:T(2,128)S(1)}, f32[2,8]{1,0:T(2,128)}, u32[]{:S(2)}) copy-start(f32[2,8]{1,0:T(2,128)} %rate_ref.1) | copy-start | bytes 196
  1.5 1.0 %copy-start.5 = (f32[2,8]{1,0:T(2,128)S(1)}, f32[2,8]{1,0:T(2,128)}, u32[]{:S(2)}) copy-start(f32[2,8]{1,0:T(2,128)} %bias_ref.1) | copy-start | bytes 196
  1.5 1.0 %copy-start.6 = (f32[8]{0:T(128)S(1)}, f32[8]{0:T(128)}, u32[]{:S(2)}) copy-start(f32[8]{0:T(128)} %param.17) | copy-start | bytes 100
  2.5 0.9 %copy-start.1 = (bf16[256,256]{1,0:T(8,128)(2,1)S(1)}, bf16[256,256]{1,0:T(8,128)(2,1)}, u32[]{:S(2)}) copy-start(bf16[256,256]{1,0:T(8,128)(2,1)} %og_ref.1) | copy-start | bytes 393220
